TPU v7x, 32 devices: a whole 2x2x4 slice. The times are simulated.
32 devices in a mesh: dp: 4 (over z), seq: 8 (over y, x, core).
Axes of the slice: x: 2, y: 2, z: 4, core: 2. Of those that a mesh axis runs over, the one named last changes fastest.
Arguments:
- tokens: bfloat16 [4, 12288, 1024], P('dp', 'seq'), may hold values from -6 to 6
- image_tokens: bfloat16 [4, 1024, 768], P('dp', 'seq'), may hold values from -51 to 51
- norm_gain: float32 [1024], replicated, may hold values from 0.1 to 1.9
- w_query: bfloat16 [1024, 1024], replicated, may hold values from -0.1875 to 0.1875
- w_key: bfloat16 [768, 1024], replicated, may hold values from -0.21875 to 0.21875
- w_value: bfloat16 [768, 1024], replicated, may hold values from -0.21875 to 0.21875
- w_out: bfloat16 [1024, 1024], replicated, may hold values from -0.1875 to 0.1875
- w_plane: bfloat16 [1024, 80], replicated, may hold values from -0.1875 to 0.1875
- dec_w1: bfloat16 [64, 80], replicated, may hold values from -0.625 to 0.625
- dec_b1: float32 [64], replicated, may hold values from -3 to 3
- dec_w2: bfloat16 [64, 64], replicated, may hold values from -0.75 to 0.75
- dec_b2: float32 [64], replicated, may hold values from -3 to 3
- dec_w3: bfloat16 [4, 64], replicated, may hold values from -0.75 to 0.75
- dec_b3: float32 [4], replicated, may hold values from -3 to 3
- corner_idx: int32 [4, 12, 32768], P('dp', None, 'seq'), may hold values from 0 to 12287, as said below
- corner_wts: bfloat16 [4, 12, 32768], P('dp', None, 'seq'), may hold values from 0 to 1, as said below
- target_color: float32 [4, 3, 256], P('dp', None, 'seq'), may hold values from 0 to 1
Outputs:
- colors: float32 [4, 3, 256], P('dp', None, 'seq')
- token_grad: bfloat16 [4, 12288, 1024], P('dp', 'seq')
- plane_weight_grad: float32 [1024, 80], replicated
Inputs may be any that keep to these rules, and one draw needn't show every extreme that they name: `corner_idx`: each entry names a triplane token of the scene; for each sample and plane the four entries are the corners of one grid cell of that plane, and consecutive samples of a ray walk through neighbouring cells. `corner_wts`: for each sample and plane the four weights are the bilinear weights of one point in that cell.
All inputs are finite; a program needn't handle non-finite values.
Results may differ from a plain program's by a relative error of at most 0.017.
Values may be sent and summed in bfloat16 or wider, within the bound.
No kernel may reach another device: no remote copies, remote signals or barrier semaphores. Data moves between devices by JAX's collectives and lax.ppermute only.
A program may use at most 128 MiB of HBM per device.

v0:
```python
import math

import jax
import jax.numpy as jnp
from jax import lax
from jax.sharding import PartitionSpec as P

HEADS = 16
STEPS = 128


NORM_EPS = 1e-05
DEPTH_STEP = 0.02


def plain_norm(inputs):
    row_mean = jnp.mean(inputs, axis=-1, keepdims=True)
    centred = inputs - row_mean
    row_var = jnp.mean(centred * centred, axis=-1, keepdims=True)
    return centred * lax.rsqrt(row_var + NORM_EPS)


def render(features, dec_w1, dec_b1, dec_w2, dec_b2, dec_w3, dec_b3):
    hidden = jax.nn.silu(
        jnp.dot(dec_w1, features, preferred_element_type=jnp.float32) + dec_b1[:, None]
    ).astype(jnp.bfloat16)
    hidden = jax.nn.silu(
        jnp.dot(dec_w2, hidden, preferred_element_type=jnp.float32) + dec_b2[:, None]
    ).astype(jnp.bfloat16)
    decoded = jnp.dot(dec_w3, hidden, preferred_element_type=jnp.float32) + dec_b3[:, None]
    optical = jax.nn.softplus(decoded[0]).reshape(-1, STEPS) * DEPTH_STEP
    albedo = jax.nn.sigmoid(decoded[1:4]).reshape(3, -1, STEPS)
    before = jnp.cumsum(optical, axis=1) - optical
    weight = jnp.exp(-before) * (1.0 - jnp.exp(-optical))
    return jnp.sum(weight[None] * albedo, axis=2)


def body(
    tokens,
    image_tokens,
    norm_gain,
    w_query,
    w_key,
    w_value,
    w_out,
    w_plane,
    dec_w1,
    dec_b1,
    dec_w2,
    dec_b2,
    dec_w3,
    dec_b3,
    corner_idx,
    corner_wts,
    target_color,
):
    own_tokens = tokens[0]
    images = image_tokens[0]
    index_table = corner_idx[0]
    weight_table = corner_wts[0]
    target = target_color[0]
    rows_here, model_width = own_tokens.shape
    head_dim = model_width // HEADS
    score_scale = 1.0 / math.sqrt(head_dim)
    image_rows = images.shape[0]
    normed = plain_norm(own_tokens.astype(jnp.float32)).astype(jnp.bfloat16)
    queries = jnp.dot(normed, w_query, preferred_element_type=jnp.float32).astype(jnp.bfloat16)
    query_heads = queries.reshape(rows_here, HEADS, head_dim)

    def attend(partial_value, key_rows, values):
        running_max, prob_sum, weighted = partial_value
        piece_rows = key_rows.shape[0]
        key_heads = key_rows.reshape(piece_rows, HEADS, head_dim)
        value_heads = values.reshape(piece_rows, HEADS, head_dim)
        scores = (
            jnp.einsum("thd,bhd->htb", query_heads, key_heads, preferred_element_type=jnp.float32)
            * score_scale
        )
        new_max = jnp.maximum(running_max, jnp.max(scores, axis=2))
        factor = jnp.exp(running_max - new_max)
        exp_terms = jnp.exp(scores - new_max[:, :, None])
        prob_sum = prob_sum * factor + jnp.sum(exp_terms, axis=2)
        weighted = weighted * factor[:, :, None] + jnp.einsum(
            "htb,bhd->htd",
            exp_terms.astype(jnp.bfloat16),
            value_heads,
            preferred_element_type=jnp.float32,
        )
        return (new_max, prob_sum, weighted)

    initial = (
        jnp.full((HEADS, rows_here), -1e30, jnp.float32),
        jnp.zeros((HEADS, rows_here), jnp.float32),
        jnp.zeros((HEADS, rows_here, head_dim), jnp.float32),
    )
    piece = lax.all_gather(images, "seq", axis=0, tiled=True)
    key_rows = jnp.dot(piece, w_key, preferred_element_type=jnp.float32).astype(jnp.bfloat16)
    values = jnp.dot(piece, w_value, preferred_element_type=jnp.float32).astype(jnp.bfloat16)
    partial_value = initial
    piece_rows = key_rows.shape[0]
    block_count = piece_rows // image_rows

    def in_advance(state_now, pair):
        return (attend(state_now, pair[0], pair[1]), None)

    partial_value, _ = lax.scan(
        in_advance,
        partial_value,
        (
            key_rows.reshape(block_count, image_rows, -1),
            values.reshape(block_count, image_rows, -1),
        ),
    )
    running_max, prob_sum, weighted = partial_value
    attended = (
        (weighted / prob_sum[:, :, None])
        .transpose(1, 0, 2)
        .reshape(rows_here, model_width)
        .astype(jnp.bfloat16)
    )
    mixed = (
        own_tokens.astype(jnp.float32)
        + jnp.dot(attended, w_out, preferred_element_type=jnp.float32)
    ).astype(jnp.bfloat16)
    plane_in = (plain_norm(mixed.astype(jnp.float32)) * norm_gain).astype(jnp.bfloat16)
    planes = lax.dot_general(
        w_plane, plane_in, (((0,), (1,)), ((), ())), preferred_element_type=jnp.float32
    ).astype(jnp.bfloat16)
    samples = index_table.shape[1]
    channels = planes.shape[0]

    def interp(offset, width_rows):
        row_ids = offset + lax.broadcasted_iota(jnp.int32, (width_rows, samples), 0)
        interp_table = jnp.zeros((width_rows, samples), jnp.bfloat16)
        for corner in range(index_table.shape[0]):
            interp_table = interp_table + jnp.where(
                row_ids == index_table[corner][None, :],
                weight_table[corner][None, :],
                jnp.zeros((), jnp.bfloat16),
            )
        return interp_table

    piece = lax.all_gather(planes, "seq", axis=1, tiled=True)
    piece_rows = piece.shape[1]
    block_count = piece_rows // rows_here

    def fold_advance(block_id, state_now):
        block_start = block_id * rows_here
        segment = lax.dynamic_slice_in_dim(piece, block_start, rows_here, 1)
        return state_now + jnp.dot(
            segment, interp(block_start, rows_here), preferred_element_type=jnp.float32
        )

    features = lax.fori_loop(
        0, block_count, fold_advance, jnp.zeros((channels, samples), jnp.float32)
    ).astype(jnp.bfloat16)

    def shade_rays(feature_in):
        return render(feature_in, dec_w1, dec_b1, dec_w2, dec_b2, dec_w3, dec_b3)

    colors, pullback = jax.vjp(shade_rays, features)
    feat_grad = pullback(colors - target)[0]

    def grad_block(block_id):
        return lax.dot_general(
            feat_grad,
            interp(block_id * rows_here, rows_here),
            (((1,), (1,)), ((), ())),
            preferred_element_type=jnp.float32,
        )

    grad_terms = lax.map(grad_block, jnp.arange(lax.axis_size("seq"), dtype=jnp.int32))
    summed = lax.psum(grad_terms.astype(jnp.bfloat16), "seq").astype(jnp.float32)
    own_grad = lax.dynamic_index_in_dim(summed, lax.axis_index("seq"), 0, keepdims=False)
    own_grad = own_grad.astype(jnp.bfloat16)
    weight_grad = lax.dot_general(
        plane_in, own_grad, (((0,), (1,)), ((), ())), preferred_element_type=jnp.float32
    )
    weight_grad = lax.psum(weight_grad, ("dp", "seq"))
    token_grad = lax.dot_general(
        own_grad, w_plane, (((0,), (1,)), ((), ())), preferred_element_type=jnp.float32
    ).astype(jnp.bfloat16)
    return (colors[None], token_grad[None], weight_grad)


def solution(mesh):
    in_specs = (
        P("dp", "seq", None),
        P("dp", "seq", None),
        P(),
        P(),
        P(),
        P(),
        P(),
        P(),
        P(),
        P(),
        P(),
        P(),
        P(),
        P(),
        P("dp", None, "seq"),
        P("dp", None, "seq"),
        P("dp", None, "seq"),
    )
    out_specs = (P("dp", None, "seq"), P("dp", "seq", None), P())
    return jax.shard_map(body, mesh=mesh, in_specs=in_specs, out_specs=out_specs, check_vma=False)
```

profile of v0, /device:TPU:1, one launch (start us, length us, event | category | flops | bytes accessed | tf_op | source)
XLA Modules:
  0.0 1254.6 jit_solution(11037289428418089711)
XLA Ops:
  23.1 15.0 %all-gather.6.cloned.1.call-done = bf16[1,1024,768]{2,1,0:T(8,128)(2,1)} async-done(((bf16[1,128,768]{2,1,0:T(8,128)(2,1)}), bf16[1,1024,768]{2,1,0:T(8,128)(2,1)}) %all-gather.6.cloned.1.call-update) | async-done | bytes 1572880 | tf_op jit(solution)/shard_map/all_gather | solution.py:96
  46.5 227.8 %while.40 = (s32[]{:T(128)}, f32[16,1536]{1,0:T(8,128)S(1)}, f32[16,1536]{1,0:T(8,128)S(1)}, f32[16,1536,64]{1,2,0:T(8,128)}, bf16[8,128,1024]{2,1,0:T(8,128)(2,...) while((s32[]{:T(128)}, f32[16,1536]{1,0:T(8,128)S(1)}, ...), condition=%wide.region_5.6_spmd.clone, body=%wide.region_2.5_spmd.clone.sunk | while | flops 835313664 | bytes 57671784 | solution.py:106
  118.9 12.0 fusion.204
  286.2 27.3 %all-gather.4.cloned.1.call-done = bf16[80,12288]{1,0:T(8,128)(2,1)} async-done(((bf16[80,1536]{1,0:T(8,128)(2,1)}), bf16[80,12288]{1,0:T(8,128)(2,1)}) %all-gather.4.cloned.1.call-update) | async-done | bytes 1966096 | tf_op jit(solution)/shard_map/all_gather | solution.py:143
  313.4 348.6 %while.41 = (s32[]{:T(128)}, f32[80,4096]{1,0:T(8,128)}, bf16[80,12288]{1,0:T(8,128)(2,1)}, s32[12,4096]{1,0:T(8,128)S(1)}, bf16[12,4096]{1,0:T(8,128)(2,1)S(1)}...) while((s32[]{:T(128)}, f32[80,4096]{1,0:T(8,128)}, bf16[80,12288]{1,0:T(8,128)(2,1)}, ...), condition=%wide.region_9.10_spmd.clone, body=%wide.region_8.9_spmd.clone.sunk | while | flops 1227490816 | bytes 3764381 | solution.py:154
  314.6 42.4 %fusion.208 = f32[80,4096]{1,0:T(8,128)} fusion(s32[4096]{0:T(1024)S(1)} %bitcast.234, s32[4096]{0:T(1024)S(1)} %bitcast.235, s32[4096]{0:T(1024)S(1)} %bitcast.236, s32[4096]{0:T(1024)S(1)} %bitcast.237, s32[4096]{0:T(1024)S(1)} %bitcast.238, s32[4096]{0:T(1024)S(1)} %bitcast.239, s32[4096]{0:T(1024)S(1)} %bitcast.240, s32[4096]{0:T(1024)S(1)} %bitcast.241, ...), kind=kOutput, calls=%fused_computation.109.clone.1 | convolution fusion | flops 1227489280 | bytes 3168261 | tf_op jit(solution)/shard_map/while/body/eval_jaxpr/dot_general | solution.py:150
  357.6 42.9 %fusion.208 = f32[80,4096]{1,0:T(8,128)} fusion(s32[4096]{0:T(1024)S(1)} %bitcast.234, s32[4096]{0:T(1024)S(1)} %bitcast.235, s32[4096]{0:T(1024)S(1)} %bitcast.236, s32[4096]{0:T(1024)S(1)} %bitcast.237, s32[4096]{0:T(1024)S(1)} %bitcast.238, s32[4096]{0:T(1024)S(1)} %bitcast.239, s32[4096]{0:T(1024)S(1)} %bitcast.240, s32[4096]{0:T(1024)S(1)} %bitcast.241, ...), kind=kOutput, calls=%fused_computation.109.clone.1 | convolution fusion | flops 1227489280 | bytes 3168261 | tf_op jit(solution)/shard_map/while/body/eval_jaxpr/dot_general | solution.py:150
  401.2 42.9 %fusion.208 = f32[80,4096]{1,0:T(8,128)} fusion(s32[4096]{0:T(1024)S(1)} %bitcast.234, s32[4096]{0:T(1024)S(1)} %bitcast.235, s32[4096]{0:T(1024)S(1)} %bitcast.236, s32[4096]{0:T(1024)S(1)} %bitcast.237, s32[4096]{0:T(1024)S(1)} %bitcast.238, s32[4096]{0:T(1024)S(1)} %bitcast.239, s32[4096]{0:T(1024)S(1)} %bitcast.240, s32[4096]{0:T(1024)S(1)} %bitcast.241, ...), kind=kOutput, calls=%fused_computation.109.clone.1 | convolution fusion | flops 1227489280 | bytes 3168261 | tf_op jit(solution)/shard_map/while/body/eval_jaxpr/dot_general | solution.py:150
  444.8 42.9 %fusion.208 = f32[80,4096]{1,0:T(8,128)} fusion(s32[4096]{0:T(1024)S(1)} %bitcast.234, s32[4096]{0:T(1024)S(1)} %bitcast.235, s32[4096]{0:T(1024)S(1)} %bitcast.236, s32[4096]{0:T(1024)S(1)} %bitcast.237, s32[4096]{0:T(1024)S(1)} %bitcast.238, s32[4096]{0:T(1024)S(1)} %bitcast.239, s32[4096]{0:T(1024)S(1)} %bitcast.240, s32[4096]{0:T(1024)S(1)} %bitcast.241, ...), kind=kOutput, calls=%fused_computation.109.clone.1 | convolution fusion | flops 1227489280 | bytes 3168261 | tf_op jit(solution)/shard_map/while/body/eval_jaxpr/dot_general | solution.py:150
  488.3 42.9 %fusion.208 = f32[80,4096]{1,0:T(8,128)} fusion(s32[4096]{0:T(1024)S(1)} %bitcast.234, s32[4096]{0:T(1024)S(1)} %bitcast.235, s32[4096]{0:T(1024)S(1)} %bitcast.236, s32[4096]{0:T(1024)S(1)} %bitcast.237, s32[4096]{0:T(1024)S(1)} %bitcast.238, s32[4096]{0:T(1024)S(1)} %bitcast.239, s32[4096]{0:T(1024)S(1)} %bitcast.240, s32[4096]{0:T(1024)S(1)} %bitcast.241, ...), kind=kOutput, calls=%fused_computation.109.clone.1 | convolution fusion | flops 1227489280 | bytes 3168261 | tf_op jit(solution)/shard_map/while/body/eval_jaxpr/dot_general | solution.py:150
  531.9 42.9 %fusion.208 = f32[80,4096]{1,0:T(8,128)} fusion(s32[4096]{0:T(1024)S(1)} %bitcast.234, s32[4096]{0:T(1024)S(1)} %bitcast.235, s32[4096]{0:T(1024)S(1)} %bitcast.236, s32[4096]{0:T(1024)S(1)} %bitcast.237, s32[4096]{0:T(1024)S(1)} %bitcast.238, s32[4096]{0:T(1024)S(1)} %bitcast.239, s32[4096]{0:T(1024)S(1)} %bitcast.240, s32[4096]{0:T(1024)S(1)} %bitcast.241, ...), kind=kOutput, calls=%fused_computation.109.clone.1 | convolution fusion | flops 1227489280 | bytes 3168261 | tf_op jit(solution)/shard_map/while/body/eval_jaxpr/dot_general | solution.py:150
  575.4 42.9 %fusion.208 = f32[80,4096]{1,0:T(8,128)} fusion(s32[4096]{0:T(1024)S(1)} %bitcast.234, s32[4096]{0:T(1024)S(1)} %bitcast.235, s32[4096]{0:T(1024)S(1)} %bitcast.236, s32[4096]{0:T(1024)S(1)} %bitcast.237, s32[4096]{0:T(1024)S(1)} %bitcast.238, s32[4096]{0:T(1024)S(1)} %bitcast.239, s32[4096]{0:T(1024)S(1)} %bitcast.240, s32[4096]{0:T(1024)S(1)} %bitcast.241, ...), kind=kOutput, calls=%fused_computation.109.clone.1 | convolution fusion | flops 1227489280 | bytes 3168261 | tf_op jit(solution)/shard_map/while/body/eval_jaxpr/dot_general | solution.py:150
  619.0 42.9 %fusion.208 = f32[80,4096]{1,0:T(8,128)} fusion(s32[4096]{0:T(1024)S(1)} %bitcast.234, s32[4096]{0:T(1024)S(1)} %bitcast.235, s32[4096]{0:T(1024)S(1)} %bitcast.236, s32[4096]{0:T(1024)S(1)} %bitcast.237, s32[4096]{0:T(1024)S(1)} %bitcast.238, s32[4096]{0:T(1024)S(1)} %bitcast.239, s32[4096]{0:T(1024)S(1)} %bitcast.240, s32[4096]{0:T(1024)S(1)} %bitcast.241, ...), kind=kOutput, calls=%fused_computation.109.clone.1 | convolution fusion | flops 1227489280 | bytes 3168261 | tf_op jit(solution)/shard_map/while/body/eval_jaxpr/dot_general | solution.py:150
  674.2 380.2 %while.39 = (s32[]{:T(128)}, bf16[8,80,1536]{2,1,0:T(8,128)(2,1)}, s32[8]{0:T(128)S(1)}, s32[12,4096]{1,0:T(8,128)S(1)}, bf16[12,4096]{1,0:T(8,128)(2,1)S(1)}, /...) while((s32[]{:T(128)}, bf16[8,80,1536]{2,1,0:T(8,128)(2,1)}, s32[8]{0:T(128)S(1)}, ...), condition=%wide.region_15.16_spmd, body=%wide.region_14.15_spmd.sunk | while | flops 1226835456 | bytes 2044529 | solution.py:172
  676.4 45.6 %fusion.197 = bf16[8,80,1536]{2,1,0:T(8,128)(2,1)} fusion(bf16[8,80,1536]{2,1,0:T(8,128)(2,1)} %get-tuple-element.599, s32[]{:T(128)} %get-tuple-element.598, bf16[80,4096]{1,0:T(8,128)(2,1)} %get-tuple-element.611, s32[4096]{0:T(1024)S(1)} %bitcast.246, s32[4096]{0:T(1024)S(1)} %bitcast.247, s32[4096]{0:T(1024)S(1)} %bitcast.248, ...), kind=kOutput, calls=%fused_computation.56.clone.1 | convolution fusion | flops 1226833920 | bytes 1448448 | tf_op jit(solution)/shard_map/while/body/eval_jaxpr/dot_general | solution.py:165
  723.9 45.6 %fusion.197 = bf16[8,80,1536]{2,1,0:T(8,128)(2,1)} fusion(bf16[8,80,1536]{2,1,0:T(8,128)(2,1)} %get-tuple-element.599, s32[]{:T(128)} %get-tuple-element.598, bf16[80,4096]{1,0:T(8,128)(2,1)} %get-tuple-element.611, s32[4096]{0:T(1024)S(1)} %bitcast.246, s32[4096]{0:T(1024)S(1)} %bitcast.247, s32[4096]{0:T(1024)S(1)} %bitcast.248, ...), kind=kOutput, calls=%fused_computation.56.clone.1 | convolution fusion | flops 1226833920 | bytes 1448448 | tf_op jit(solution)/shard_map/while/body/eval_jaxpr/dot_general | solution.py:165
  771.4 45.6 %fusion.197 = bf16[8,80,1536]{2,1,0:T(8,128)(2,1)} fusion(bf16[8,80,1536]{2,1,0:T(8,128)(2,1)} %get-tuple-element.599, s32[]{:T(128)} %get-tuple-element.598, bf16[80,4096]{1,0:T(8,128)(2,1)} %get-tuple-element.611, s32[4096]{0:T(1024)S(1)} %bitcast.246, s32[4096]{0:T(1024)S(1)} %bitcast.247, s32[4096]{0:T(1024)S(1)} %bitcast.248, ...), kind=kOutput, calls=%fused_computation.56.clone.1 | convolution fusion | flops 1226833920 | bytes 1448448 | tf_op jit(solution)/shard_map/while/body/eval_jaxpr/dot_general | solution.py:165
  818.8 45.6 %fusion.197 = bf16[8,80,1536]{2,1,0:T(8,128)(2,1)} fusion(bf16[8,80,1536]{2,1,0:T(8,128)(2,1)} %get-tuple-element.599, s32[]{:T(128)} %get-tuple-element.598, bf16[80,4096]{1,0:T(8,128)(2,1)} %get-tuple-element.611, s32[4096]{0:T(1024)S(1)} %bitcast.246, s32[4096]{0:T(1024)S(1)} %bitcast.247, s32[4096]{0:T(1024)S(1)} %bitcast.248, ...), kind=kOutput, calls=%fused_computation.56.clone.1 | convolution fusion | flops 1226833920 | bytes 1448448 | tf_op jit(solution)/shard_map/while/body/eval_jaxpr/dot_general | solution.py:165
  866.4 45.5 %fusion.197 = bf16[8,80,1536]{2,1,0:T(8,128)(2,1)} fusion(bf16[8,80,1536]{2,1,0:T(8,128)(2,1)} %get-tuple-element.599, s32[]{:T(128)} %get-tuple-element.598, bf16[80,4096]{1,0:T(8,128)(2,1)} %get-tuple-element.611, s32[4096]{0:T(1024)S(1)} %bitcast.246, s32[4096]{0:T(1024)S(1)} %bitcast.247, s32[4096]{0:T(1024)S(1)} %bitcast.248, ...), kind=kOutput, calls=%fused_computation.56.clone.1 | convolution fusion | flops 1226833920 | bytes 1448448 | tf_op jit(solution)/shard_map/while/body/eval_jaxpr/dot_general | solution.py:165
  913.8 45.6 %fusion.197 = bf16[8,80,1536]{2,1,0:T(8,128)(2,1)} fusion(bf16[8,80,1536]{2,1,0:T(8,128)(2,1)} %get-tuple-element.599, s32[]{:T(128)} %get-tuple-element.598, bf16[80,4096]{1,0:T(8,128)(2,1)} %get-tuple-element.611, s32[4096]{0:T(1024)S(1)} %bitcast.246, s32[4096]{0:T(1024)S(1)} %bitcast.247, s32[4096]{0:T(1024)S(1)} %bitcast.248, ...), kind=kOutput, calls=%fused_computation.56.clone.1 | convolution fusion | flops 1226833920 | bytes 1448448 | tf_op jit(solution)/shard_map/while/body/eval_jaxpr/dot_general | solution.py:165
  961.3 45.6 %fusion.197 = bf16[8,80,1536]{2,1,0:T(8,128)(2,1)} fusion(bf16[8,80,1536]{2,1,0:T(8,128)(2,1)} %get-tuple-element.599, s32[]{:T(128)} %get-tuple-element.598, bf16[80,4096]{1,0:T(8,128)(2,1)} %get-tuple-element.611, s32[4096]{0:T(1024)S(1)} %bitcast.246, s32[4096]{0:T(1024)S(1)} %bitcast.247, s32[4096]{0:T(1024)S(1)} %bitcast.248, ...), kind=kOutput, calls=%fused_computation.56.clone.1 | convolution fusion | flops 1226833920 | bytes 1448448 | tf_op jit(solution)/shard_map/while/body/eval_jaxpr/dot_general | solution.py:165
  1008.8 45.6 %fusion.197 = bf16[8,80,1536]{2,1,0:T(8,128)(2,1)} fusion(bf16[8,80,1536]{2,1,0:T(8,128)(2,1)} %get-tuple-element.599, s32[]{:T(128)} %get-tuple-element.598, bf16[80,4096]{1,0:T(8,128)(2,1)} %get-tuple-element.611, s32[4096]{0:T(1024)S(1)} %bitcast.246, s32[4096]{0:T(1024)S(1)} %bitcast.247, s32[4096]{0:T(1024)S(1)} %bitcast.248, ...), kind=kOutput, calls=%fused_computation.56.clone.1 | convolution fusion | flops 1226833920 | bytes 1448448 | tf_op jit(solution)/shard_map/while/body/eval_jaxpr/dot_general | solution.py:165
  1054.4 59.4 %all-reduce.5.cloned.1.call-done = bf16[8,80,1536]{2,1,0:T(8,128)(2,1)} async-done(((bf16[8,80,1536]{2,1,0:T(8,128)(2,1)}), bf16[8,80,1536]{2,1,0:T(8,128)(2,1)}) %all-reduce.5.cloned.1.call-update) | async-done | bytes 1966096 | tf_op jit(solution)/shard_map/psum | solution.py:173
  1121.9 124.2 %all-reduce.7.cloned.1.call-done = f32[1024,80]{0,1:T(8,128)} async-done(((f32[1024,80]{0,1:T(8,128)}), f32[1024,80]{0,1:T(8,128)}) %all-reduce.7.cloned.1.call-update) | async-done | bytes 327696 | tf_op jit(solution)/shard_map/psum | solution.py:179
  (234 shorter events, 288.4 us)
Async XLA Ops:
  7.2 271.0 %copy-start = (bf16[1024,1024]{1,0:T(8,128)(2,1)S(1)}, bf16[1024,1024]{1,0:T(8,128)(2,1)}, u32[]{:S(2)}) copy-start(bf16[1024,1024]{1,0:T(8,128)(2,1)} %param.29) | copy-start | bytes 6291460
  7.2 31.0 %all-gather.6.cloned.1.call-start = ((), (), s32[]{:S(2)}) async-start(), calls=%async_computation.3 | async-start | bytes 1769472 | tf_op jit(solution)/shard_map/all_gather | solution.py:96
  7.9 305.5 %all-gather.4.cloned.1.call-start = ((), (), s32[]{:S(2)}) async-start(), calls=%async_computation | async-start | bytes 2211840 | tf_op jit(solution)/shard_map/all_gather | solution.py:143
  12.6 5.3 copy-start.2
  12.6 5.3 copy-start.19
  38.2 5.2 copy-start.20
  38.2 5.2 copy-start.21
  274.3 3.8 copy-start.3
  278.2 5.8 copy-start.7
  278.2 5.8 copy-start.23
  282.3 3.7 copy-start.6
  282.4 31.1 %copy-start.1 = (bf16[1,12,4096]{2,1,0:T(8,128)(2,1)S(1)}, bf16[1,12,4096]{2,1,0:T(8,128)(2,1)}, u32[]{:S(2)}) copy-start(bf16[1,12,4096]{2,1,0:T(8,128)(2,1)} %param.38) | copy-start | bytes 294916
  285.9 828.0 %all-reduce.5.cloned.1.call-start = ((), (), s32[]{:S(2)}) async-start(), calls=%async_computation.1 | async-start | bytes 3932160 | tf_op jit(solution)/shard_map/psum | solution.py:173
  313.4 348.6 %copy-start.13 = (bf16[64,80]{1,0:T(8,128)(2,1)S(1)}, bf16[64,80]{1,0:T(8,128)(2,1)}, u32[]{:S(2)}) copy-start(bf16[64,80]{1,0:T(8,128)(2,1)} %param.31) | copy-start | bytes 30724
  313.4 348.6 %copy-start.18 = (f32[64]{0:T(128)S(1)}, f32[64]{0:T(128)}, u32[]{:S(2)}) copy-start(f32[64]{0:T(128)} %param.32) | copy-start | bytes 772
  313.4 351.2 %copy-start.22 = (bf16[64,64]{1,0:T(8,128)(2,1)S(1)}, bf16[64,64]{1,0:T(8,128)(2,1)}, u32[]{:S(2)}) copy-start(bf16[64,64]{1,0:T(8,128)(2,1)} %param.33) | copy-start | bytes 24580
  313.4 351.2 %copy-start.25 = (f32[64]{0:T(128)S(1)}, f32[64]{0:T(128)}, u32[]{:S(2)}) copy-start(f32[64]{0:T(128)} %param.34) | copy-start | bytes 772
  662.0 5.2 copy-start.16
  674.2 439.7 %copy-start.10 = (f32[1536]{0:T(1024)S(1)}, f32[1536]{0:T(1024)}, u32[]{:S(2)}) copy-start(f32[1536]{0:T(1024)} %copy-done.9) | copy-start | bytes 18436
  674.2 439.7 %copy-start.15 = (f32[1536]{0:T(1024)S(1)}, f32[1536]{0:T(1024)}, u32[]{:S(2)}) copy-start(f32[1536]{0:T(1024)} %copy-done.14) | copy-start | bytes 18436
  674.2 439.7 %copy-start.24 = (f32[1024]{0:T(1024)S(1)}, f32[1024]{0:T(1024)}, u32[]{:S(2)}) copy-start(f32[1024]{0:T(1024)} %param.25) | copy-start | bytes 12292
  1054.4 63.4 %copy-start.12 = (f32[3,32]{1,0:T(4,128)S(1)}, f32[3,32]{1,0:T(4,128)}, u32[]{:S(2)}) copy-start(f32[3,32]{1,0:T(4,128)} %copy-done.11) | copy-start | bytes 1156
  1054.4 64.0 %copy-start.8 = (bf16[1024,80]{0,1:T(8,128)(2,1)S(1)}, bf16[1024,80]{0,1:T(8,128)(2,1)}, u32[]{:S(2)}) copy-start(bf16[1024,80]{0,1:T(8,128)(2,1)} %param.30) | copy-start | bytes 491524
  1054.4 191.7 %all-reduce.7.cloned.1.call-start = ((), (), s32[]{:S(2)}) async-start(), calls=%async_computation.2 | async-start | bytes 655360 | tf_op jit(solution)/shard_map/psum | solution.py:179
  (8 other events, 16.1 us)
Sparse Core Ops, SparseCore 0:
  9.9 28.2 all-gather.5
  286.0 27.3 all-gather.3
  1054.5 59.3 all-reduce.4
  1119.7 126.3 all-reduce.6
where the time goes:
time: 1260 us; the launch traced here: 1250 us
  matrix products  902 us (72%)
  waiting for transfers between devices  227 us (18%)
  other arithmetic  68 us (5%)
  local copies, waits for them, and re-layouts  36.6 us (3%)
  between operations  14.4 us (1%)
    dot_general x8, matrix products, grad_block(): lax.dot_general(feat_grad, interp(block_id * rows_here, rows_here), (((1,...  365 us
    dot_general x8, matrix products, fold_advance(): jnp.dot(segment, interp(block_start, rows_here), preferred_element_type=j...  342 us
    psum x1, waiting for transfers between devices, body(): weight_grad = lax.psum(weight_grad, ('dp', 'seq'))  124 us
    dot_general x8, matrix products, attend(): jnp.einsum('htb,bhd->htd', exp_terms.astype(jnp.bfloat16), value_heads, p...  94.3 us
    dot_general x8, matrix products, attend(): jnp.einsum('thd,bhd->htb', query_heads, key_heads, preferred_element_type...  66.5 us
    psum x1, waiting for transfers between devices, body(): lax.psum(grad_terms.astype(jnp.bfloat16), 'seq').astype(jnp.float32)  59.4 us
    reduce_sum x8, other arithmetic, attend(): prob_sum = prob_sum * factor + jnp.sum(exp_terms, axis=2)  54.6 us
    all_gather x1, waiting for transfers between devices, body(): piece = lax.all_gather(planes, 'seq', axis=1, tiled=True)  27.3 us
  transfers between devices with their start and end apart: 4, of which 4 were waited for; matrix products, arithmetic and copies ran while one was open for 2% of the time, Pallas kernels for 0%

commit v1 on v0

v1 whole, which is shorter than its diff:
```python
import functools
import math

import jax
import jax.numpy as jnp
from jax import lax
from jax.experimental import pallas as pl
from jax.experimental.pallas import tpu as pltpu
from jax.sharding import PartitionSpec as P

HEADS = 16
STEPS = 128
PLANES = 3
LANES = 128

NORM_EPS = 1e-05
DEPTH_STEP = 0.02
VMEM_BYTES = 56 * 1024 * 1024

F32 = jnp.float32
BF16 = jnp.bfloat16


def contract(left, right, left_dim, right_dim, out_type=F32, precision=None):
    return lax.dot_general(
        left,
        right,
        (((left_dim,), (right_dim,)), ((), ())),
        preferred_element_type=out_type,
        precision=precision,
    )


def plain_norm(inputs):
    row_mean = jnp.mean(inputs, axis=-1, keepdims=True)
    centred = inputs - row_mean
    row_var = jnp.mean(centred * centred, axis=-1, keepdims=True)
    return centred * lax.rsqrt(row_var + NORM_EPS)


def params(steps=1):
    return pltpu.CompilerParams(
        vmem_limit_bytes=VMEM_BYTES, dimension_semantics=("arbitrary",) * steps
    )


def swap(array, axis, distance):
    pairs = [(i, i ^ distance) for i in range(lax.axis_size(axis))]
    return lax.ppermute(array, axis, pairs)


def gather_scene(piece):
    far = [piece] + [swap(piece, "seq", k) for k in range(2, lax.axis_size("seq"), 2)]
    pieces = []
    for own_side in far:
        pieces += [own_side, swap(own_side, "seq", 1)]
    return pieces


def whole(shape):
    return pl.BlockSpec(shape, lambda step: (0,) * len(shape))


def query_kernel(query_scale, tokens_ref, w_query_ref, queries_ref):
    normed = plain_norm(tokens_ref[...].astype(F32)).astype(BF16)
    queries = jnp.dot(normed, w_query_ref[...], preferred_element_type=F32)
    queries_ref[...] = (queries * query_scale).astype(BF16)


def query_call(tokens, w_query, query_scale):
    rows, width = tokens.shape
    tile = math.gcd(rows, 512)
    return pl.pallas_call(
        functools.partial(query_kernel, query_scale),
        grid=(rows // tile,),
        in_specs=[pl.BlockSpec((tile, width), lambda step: (step, 0)), whole(w_query.shape)],
        out_specs=pl.BlockSpec((tile, width), lambda step: (step, 0)),
        out_shape=jax.ShapeDtypeStruct((rows, width), BF16),
        compiler_params=params(),
        name="queries",
    )(tokens, w_query)


def keys_kernel(count, *refs):
    images_refs, (w_key_ref, w_value_ref, keys_ref, values_ref) = refs[:count], refs[count:]
    images = jnp.concatenate([ref[...] for ref in images_refs], axis=0)
    keys = jnp.dot(images, w_key_ref[...], preferred_element_type=F32).astype(BF16)
    keys_ref[...] = keys.T
    values = jnp.dot(images, w_value_ref[...], preferred_element_type=F32).astype(BF16)
    ones = jnp.ones((values.shape[0], LANES), BF16)
    for group in range(values.shape[1] // LANES):
        values_ref[group, :, :LANES] = values[:, group * LANES : (group + 1) * LANES]
        values_ref[group, :, LANES:] = ones


def keys_call(images, w_key, w_value):
    rows = sum(piece.shape[0] for piece in images)
    width = w_key.shape[1]
    return pl.pallas_call(
        functools.partial(keys_kernel, len(images)),
        out_shape=[
            jax.ShapeDtypeStruct((width, rows), BF16),
            jax.ShapeDtypeStruct((width // LANES, rows, 2 * LANES), BF16),
        ],
        compiler_params=pltpu.CompilerParams(vmem_limit_bytes=VMEM_BYTES),
        name="keys_values",
    )(*images, w_key, w_value)


def attend_kernel(
    head_dim,
    tokens_ref,
    queries_ref,
    keys_ref,
    values_ref,
    w_out_ref,
    gain_ref,
    w_plane_ref,
    plane_in_ref,
    planes_ref,
    attended_ref,
):
    rows, width = tokens_ref.shape
    lane_ids = lax.broadcasted_iota(jnp.int32, (rows, LANES), 1)

    def group_step(group, _):
        start = pl.multiple_of(group * LANES, LANES)
        columns = pl.ds(start, LANES)
        group_queries = queries_ref[:, columns]
        group_keys = keys_ref[columns, :]
        group_values = values_ref[group]
        joined = jnp.zeros((rows, LANES), F32)
        for low in range(0, LANES, head_dim):
            own = (lane_ids >= low) & (lane_ids < low + head_dim)
            head_queries = jnp.where(own, group_queries, jnp.zeros_like(group_queries))
            scores = jnp.dot(head_queries, group_keys, preferred_element_type=F32)
            row_max = jnp.max(scores, axis=1, keepdims=True)
            probs = jnp.exp2(scores - row_max).astype(BF16)
            sums = jnp.dot(probs, group_values, preferred_element_type=F32)
            joined = jnp.where(own, sums[:, :LANES] / sums[:, LANES:], joined)
        attended_ref[:, columns] = joined.astype(BF16)
        return 0

    lax.fori_loop(0, width // LANES, group_step, 0)
    mixed = (
        tokens_ref[...].astype(F32)
        + jnp.dot(attended_ref[...], w_out_ref[...], preferred_element_type=F32)
    ).astype(BF16)
    plane_in = (plain_norm(mixed.astype(F32)) * gain_ref[...]).astype(BF16)
    plane_in_ref[...] = plane_in
    planes_ref[...] = contract(w_plane_ref[...], plane_in, 1, 1).astype(BF16)


def attend_call(tokens, queries, keys, values, w_out, norm_gain, w_plane_t, head_dim):
    rows, width = tokens.shape
    channels = w_plane_t.shape[0]
    tile = math.gcd(rows, 768)
    row_block = pl.BlockSpec((tile, width), lambda step: (step, 0))
    return pl.pallas_call(
        functools.partial(attend_kernel, head_dim),
        grid=(rows // tile,),
        in_specs=[
            row_block,
            row_block,
            whole(keys.shape),
            whole(values.shape),
            whole(w_out.shape),
            whole((1, width)),
            whole(w_plane_t.shape),
        ],
        out_specs=[row_block, pl.BlockSpec((channels, tile), lambda step: (0, step))],
        out_shape=[
            jax.ShapeDtypeStruct((rows, width), BF16),
            jax.ShapeDtypeStruct((channels, rows), BF16),
        ],
        scratch_shapes=[pltpu.VMEM((tile, width), BF16)],
        compiler_params=params(),
        name="attention_planes",
    )(tokens, queries, keys, values, w_out, norm_gain.reshape(1, width), w_plane_t)


def shifted_left(block, lanes):
    return pltpu.roll(block, block.shape[1] - lanes, 1) if lanes else block


def render_kernel(
    grid_side,
    row_span,
    shares,
    *refs,
):
    piece_refs, refs = refs[:shares], refs[shares:]
    (index_ref, weight_ref, target_ref, w1_ref, b1_ref, w2_ref, b2_ref, w3_ref, b3_ref), refs = (
        refs[:9],
        refs[9:],
    )
    colors_ref, even_refs, odd_refs = refs[0], refs[1 : 1 + shares // 2], refs[1 + shares // 2 : 1 + shares]
    bands_ref, sums_ref, matrix_ref, whole_ref = refs[1 + shares :]
    step = pl.program_id(0)
    me = lax.axis_index("seq")
    channels, share = piece_refs[0].shape
    samples = index_ref.shape[1]
    corners = index_ref.shape[0]
    plane_size = grid_side * grid_side
    band_rows = row_span + 1
    band = band_rows * grid_side
    stride = row_span * grid_side
    bands = (grid_side - 1) // row_span
    rays = samples // STEPS

    @pl.when(step == 0)
    def fill_bands():
        sums_ref[...] = jnp.zeros_like(sums_ref)
        for k in range(shares):
            whole_ref[me ^ k] = piece_refs[k][...]
        whole_planes = jnp.concatenate([whole_ref[i] for i in range(shares)], axis=1)
        for plane in range(PLANES):
            for q in range(bands):
                start = plane * plane_size + q * stride
                lead = start % LANES
                extent = band + (LANES if lead else 0)
                piece = whole_planes[:, start - lead : start - lead + extent]
                if lead:
                    piece = shifted_left(piece.astype(F32), lead).astype(BF16)
                bands_ref[plane, q * channels : (q + 1) * channels, :] = piece[:, :band]

    index = index_ref[...]
    weights = weight_ref[...].astype(F32)
    features = jnp.zeros((channels, samples), F32)
    x_ids = lax.broadcasted_iota(jnp.int32, (grid_side, samples), 0)
    band_ids = []
    for plane in range(PLANES):
        in_plane = (index >= plane * plane_size) & (index < (plane + 1) * plane_size)
        base = jnp.min(jnp.where(in_plane, index, PLANES * plane_size), axis=0, keepdims=True)
        picked = [
            jnp.sum(jnp.where(index == base + shift, weights, 0.0), axis=0, keepdims=True)
            for shift in (0, 1, grid_side, grid_side + 1)
        ]
        local = base - plane * plane_size
        first_row = local // grid_side
        first_x = local - first_row * grid_side
        band_id = first_row // row_span
        band_row = first_row - band_id * row_span
        band_ids.append(band_id)
        at_first = x_ids == first_x
        at_second = x_ids == first_x + 1
        upper = jnp.where(at_first, picked[0], jnp.where(at_second, picked[1], 0.0)).astype(BF16)
        lower = jnp.where(at_first, picked[2], jnp.where(at_second, picked[3], 0.0)).astype(BF16)
        row_marks = [
            jnp.where(band_row == r, 1.0, 0.0).astype(BF16) for r in range(row_span)
        ]
        for r in range(band_rows):
            block = None
            if r < row_span:
                block = upper * row_marks[r]
            if r > 0:
                below = lower * row_marks[r - 1]
                block = below if block is None else block + below
            matrix_ref[plane, r * grid_side : (r + 1) * grid_side, :] = block
        products = jnp.dot(bands_ref[plane], matrix_ref[plane], preferred_element_type=F32)
        for q in range(bands):
            features = features + jnp.where(
                band_id == q, products[q * channels : (q + 1) * channels, :], 0.0
            )
    features = features.astype(BF16)

    pre1 = jnp.dot(w1_ref[...], features, preferred_element_type=F32) + b1_ref[...]
    gate1 = jax.nn.sigmoid(pre1)
    hidden1 = (pre1 * gate1).astype(BF16)
    pre2 = jnp.dot(w2_ref[...], hidden1, preferred_element_type=F32) + b2_ref[...]
    gate2 = jax.nn.sigmoid(pre2)
    hidden2 = (pre2 * gate2).astype(BF16)
    decoded = jnp.dot(w3_ref[...], hidden2, preferred_element_type=F32) + b3_ref[...]

    def by_ray(row):
        return jnp.concatenate(
            [decoded[row : row + 1, i * STEPS : (i + 1) * STEPS] for i in range(rays)], axis=0
        )

    def along_lanes(by_rays):
        return jnp.concatenate([by_rays[i : i + 1, :] for i in range(rays)], axis=1)

    earlier = lax.broadcasted_iota(jnp.int32, (STEPS, STEPS), 0)
    later = lax.broadcasted_iota(jnp.int32, (STEPS, STEPS), 1)
    raw_density = by_ray(0)
    density = jnp.maximum(raw_density, 0.0) + jnp.log1p(jnp.exp(-jnp.abs(raw_density)))
    optical = density * DEPTH_STEP
    before = jnp.dot(
        optical,
        jnp.where(earlier < later, 1.0, 0.0),
        preferred_element_type=F32,
        precision=lax.Precision.HIGHEST,
    )
    through = jnp.exp(-before)
    passing = jnp.exp(-optical)
    ray_weight = through * (1.0 - passing)
    target = target_ref[...]
    lane_ids = lax.broadcasted_iota(jnp.int32, (rays, LANES), 1)
    color_block = jnp.zeros((rays, LANES), F32)
    weight_slope = jnp.zeros((rays, STEPS), F32)
    decoded_slopes = []
    for channel in range(3):
        albedo = jax.nn.sigmoid(by_ray(1 + channel))
        color = jnp.sum(ray_weight * albedo, axis=1, keepdims=True)
        color_block = jnp.where(lane_ids == channel, color, color_block)
        residual = color - jnp.sum(
            jnp.where(lane_ids == channel, target, 0.0), axis=1, keepdims=True
        )
        weight_slope = weight_slope + residual * albedo
        decoded_slopes.append(along_lanes(residual * ray_weight * albedo * (1.0 - albedo)))
    colors_ref[...] = color_block
    behind = jnp.dot(
        weight_slope * ray_weight,
        jnp.where(earlier > later, 1.0, 0.0),
        preferred_element_type=F32,
        precision=lax.Precision.HIGHEST,
    )
    optical_slope = weight_slope * through * passing - behind
    density_slope = optical_slope * DEPTH_STEP * jax.nn.sigmoid(raw_density)
    decoded_slope = jnp.concatenate([along_lanes(density_slope)] + decoded_slopes, axis=0)

    hidden2_slope = contract(w3_ref[...], decoded_slope.astype(BF16), 0, 0).astype(BF16)
    pre2_slope = hidden2_slope.astype(F32) * (gate2 * (1.0 + pre2 * (1.0 - gate2)))
    hidden1_slope = contract(w2_ref[...], pre2_slope.astype(BF16), 0, 0).astype(BF16)
    pre1_slope = hidden1_slope.astype(F32) * (gate1 * (1.0 + pre1 * (1.0 - gate1)))
    feature_slope = contract(w1_ref[...], pre1_slope.astype(BF16), 0, 0).astype(BF16)

    for plane in range(PLANES):
        spread = jnp.concatenate(
            [
                feature_slope * jnp.where(band_ids[plane] == q, 1.0, 0.0).astype(BF16)
                for q in range(bands)
            ],
            axis=0,
        )
        sums_ref[plane] += contract(spread, matrix_ref[plane], 1, 1)

    @pl.when(step == pl.num_programs(0) - 1)
    def join_bands():
        joined = []
        for plane in range(PLANES):
            total = jnp.zeros((channels, plane_size), F32)
            for q in range(bands):
                start = q * stride
                lead = start % LANES
                piece = sums_ref[plane, q * channels : (q + 1) * channels, :]
                if lead:
                    piece = jnp.concatenate([piece, jnp.zeros((channels, LANES), F32)], axis=1)
                    piece = pltpu.roll(piece, lead, 1)
                parts = []
                if start - lead > 0:
                    parts.append(jnp.zeros((channels, start - lead), F32))
                parts.append(piece)
                left_over = plane_size - (start - lead) - piece.shape[1]
                if left_over > 0:
                    parts.append(jnp.zeros((channels, left_over), F32))
                total = total + jnp.concatenate(parts, axis=1)
            joined.append(total.astype(BF16))
        joined = jnp.concatenate(joined, axis=1)
        for i in range(shares):
            whole_ref[i] = joined[:, i * share : (i + 1) * share]
        for k in range(0, shares, 2):
            even_refs[k // 2][...] = whole_ref[me ^ k]
            odd_refs[k // 2][...] = whole_ref[me ^ (k + 1)]


def render_call(pieces, index, weights, target, w1, b1, w2, b2, w3, b3):
    shares = len(pieces)
    channels, share = pieces[0].shape
    corners, samples = index.shape
    grid_side = math.isqrt(shares * share // PLANES)
    row_span = next(
        span
        for span in range(7, 0, -1)
        if (grid_side - 1) % span == 0
    )
    bands = (grid_side - 1) // row_span
    band = (row_span + 1) * grid_side
    rays = samples // STEPS
    tile_rays = math.gcd(rays, 8)
    tile = tile_rays * STEPS
    padded_target = jnp.pad(target.T, ((0, 0), (0, LANES - target.shape[0])))
    column = lambda array: array.reshape(-1, 1)
    colors, *grads = pl.pallas_call(
        functools.partial(render_kernel, grid_side, row_span, shares),
        grid=(rays // tile_rays,),
        in_specs=[
            *[whole((channels, share))] * shares,
            pl.BlockSpec((corners, tile), lambda step: (0, step)),
            pl.BlockSpec((corners, tile), lambda step: (0, step)),
            pl.BlockSpec((tile_rays, LANES), lambda step: (step, 0)),
            whole(w1.shape),
            whole((w1.shape[0], 1)),
            whole(w2.shape),
            whole((w2.shape[0], 1)),
            whole(w3.shape),
            whole((w3.shape[0], 1)),
        ],
        out_specs=[
            pl.BlockSpec((tile_rays, LANES), lambda step: (step, 0)),
            *[whole((channels, share))] * shares,
        ],
        out_shape=[
            jax.ShapeDtypeStruct((rays, LANES), F32),
            *[jax.ShapeDtypeStruct((channels, share), BF16)] * shares,
        ],
        scratch_shapes=[
            pltpu.VMEM((PLANES, bands * channels, band), BF16),
            pltpu.VMEM((PLANES, bands * channels, band), F32),
            pltpu.VMEM((PLANES, band, tile), BF16),
            pltpu.VMEM((shares, channels, share), BF16),
        ],
        compiler_params=params(),
        name="render",
    )(*pieces, index, weights, padded_target, w1, column(b1), w2, column(b2), w3, column(b3))
    return colors[:, : target.shape[0]].T, grads[: shares // 2], grads[shares // 2 :]


def weight_grad_kernel(count, *refs):
    part_refs, (plane_in_ref, even_ref, odd_ref, grad_ref, chunk_ref) = refs[:count], refs[count:]
    me = lax.axis_index("seq")
    grad = part_refs[0][...].astype(F32)
    for ref in part_refs[1:]:
        grad = grad + ref[...].astype(F32)
    grad = grad.astype(BF16)
    grad_ref[...] = grad
    total = jnp.dot(grad, plane_in_ref[...], preferred_element_type=F32)
    shares, _, columns = chunk_ref.shape
    for i in range(shares):
        chunk_ref[i] = total[:, i * columns : (i + 1) * columns]
    for j in range(shares // 2):
        even_ref[j] = chunk_ref[me ^ (2 * j)]
        odd_ref[j] = chunk_ref[me ^ (2 * j + 1)]


def weight_grad_call(parts, plane_in, shares):
    rows, width = plane_in.shape
    channels = parts[0].shape[0]
    columns = width // shares
    chunks = (shares // 2, channels, columns)
    return pl.pallas_call(
        functools.partial(weight_grad_kernel, len(parts)),
        out_shape=[
            jax.ShapeDtypeStruct(chunks, F32),
            jax.ShapeDtypeStruct(chunks, F32),
            jax.ShapeDtypeStruct((channels, rows), BF16),
        ],
        scratch_shapes=[pltpu.VMEM((shares, channels, columns), F32)],
        compiler_params=pltpu.CompilerParams(vmem_limit_bytes=VMEM_BYTES),
        name="weight_grad",
    )(*parts, plane_in)


def token_grad_kernel(grad_ref, w_plane_ref, token_grad_ref):
    token_grad_ref[...] = contract(grad_ref[...], w_plane_ref[...], 0, 0).astype(BF16)


def token_grad_call(grad, w_plane_t):
    channels, rows = grad.shape
    width = w_plane_t.shape[1]
    tile = math.gcd(rows, 384)
    return pl.pallas_call(
        token_grad_kernel,
        grid=(rows // tile,),
        in_specs=[
            pl.BlockSpec((channels, tile), lambda step: (0, step)),
            whole(w_plane_t.shape),
        ],
        out_specs=pl.BlockSpec((tile, width), lambda step: (step, 0)),
        out_shape=jax.ShapeDtypeStruct((rows, width), BF16),
        cost_estimate=pl.CostEstimate(
            flops=2 * rows * width * channels, bytes_accessed=2 * rows * width, transcendentals=0
        ),
        compiler_params=params(),
        name="token_grad",
    )(grad, w_plane_t)


def join_kernel(count, *refs):
    chunk_refs, (out_ref,) = refs[:count], refs[count:]
    me = lax.axis_index("seq")
    columns = chunk_refs[0].shape[1]
    for k in range(count):
        start = pl.multiple_of((me ^ k) * columns, columns)
        out_ref[pl.ds(start, columns), :] = chunk_refs[k][...].T


def join_call(chunks):
    channels, columns = chunks[0].shape
    return pl.pallas_call(
        functools.partial(join_kernel, len(chunks)),
        out_shape=jax.ShapeDtypeStruct((columns * len(chunks), channels), F32),
        name="join_weight_grad",
    )(*chunks)


def body(
    tokens,
    image_tokens,
    norm_gain,
    w_query,
    w_key,
    w_value,
    w_out,
    w_plane,
    dec_w1,
    dec_b1,
    dec_w2,
    dec_b2,
    dec_w3,
    dec_b3,
    corner_idx,
    corner_wts,
    target_color,
):
    own_tokens = tokens[0]
    head_dim = own_tokens.shape[1] // HEADS
    query_scale = math.log2(math.e) / math.sqrt(head_dim)
    shares = lax.axis_size("seq")
    images = gather_scene(image_tokens[0])
    queries = query_call(own_tokens, w_query, query_scale)
    keys, values = keys_call(images, w_key, w_value)
    w_plane_t = w_plane.T
    plane_in, planes = attend_call(
        own_tokens, queries, keys, values, w_out, norm_gain, w_plane_t, head_dim
    )
    colors, kept, passed = render_call(
        gather_scene(planes),
        corner_idx[0],
        corner_wts[0],
        target_color[0],
        dec_w1,
        dec_b1,
        dec_w2,
        dec_b2,
        dec_w3,
        dec_b3,
    )
    parts = []
    for j in reversed(range(shares // 2)):
        pair = (kept[j].astype(F32) + swap(passed[j], "seq", 1).astype(F32)).astype(BF16)
        parts.append(swap(pair, "seq", 2 * j) if j else pair)
    kept, passed, grad = weight_grad_call(parts, plane_in, shares)
    token_grad = token_grad_call(grad, w_plane_t)
    pairs = kept + swap(passed, "seq", 1)
    chunk = pairs[0]
    for j in range(1, shares // 2):
        chunk = chunk + swap(pairs[j], "seq", 2 * j)
    scenes = chunk
    for k in range(1, lax.axis_size("dp")):
        scenes = scenes + swap(chunk, "dp", k)
    weight_grad = join_call(gather_scene(scenes))
    return (colors[None], token_grad[None], weight_grad)


def solution(mesh):
    in_specs = (
        P("dp", "seq", None),
        P("dp", "seq", None),
        P(),
        P(),
        P(),
        P(),
        P(),
        P(),
        P(),
        P(),
        P(),
        P(),
        P(),
        P(),
        P("dp", None, "seq"),
        P("dp", None, "seq"),
        P("dp", None, "seq"),
    )
    out_specs = (P("dp", None, "seq"), P("dp", "seq", None), P())
    return jax.shard_map(body, mesh=mesh, in_specs=in_specs, out_specs=out_specs, check_vma=False)
```

time: 1260 us -> 200 us (0.16)
  matrix products: 902 us -> 0 us
  waiting for transfers between devices: 227 us -> 28.5 us
  Pallas kernels: 0 us -> 114 us
  other arithmetic: 68 us -> 5.68 us
  starting transfers between devices: 0.16 us -> 39.8 us
  local copies, waits for them, and re-layouts: 36.6 us -> 10.5 us
  between operations: 14.4 us -> 0.96 us
    dot_general x44 -> x0, matrix products: 902 us -> none  [the longest x8 365 us: grad_block(): lax.dot_general(feat_grad, interp(block_id * rows_here, rows_here), (((1,...]
    psum x2 -> x0, waiting for transfers between devices: 184 us -> none  [the longest x1 124 us: body(): weight_grad = lax.psum(weight_grad, ('dp', 'seq'))]
    pallas_call x0 -> x7, Pallas kernels: none -> 114 us  [the longest x1 55.4 us: attend_call(): pl.pallas_call(functools.partial(attend_kernel, head_dim), grid=(rows //...]
    reduce_sum x12 -> x0, other arithmetic: 60.9 us -> none  [the longest x8 54.6 us: attend(): prob_sum = prob_sum * factor + jnp.sum(exp_terms, axis=2)]
    all_gather x2 -> x0, waiting for transfers between devices: 42.3 us -> none  [the longest x1 27.3 us: body(): piece = lax.all_gather(planes, 'seq', axis=1, tiled=True)]
    ppermute x0 -> x35, starting transfers between devices: none -> 39.8 us  [swap(): return lax.ppermute(array, axis, pairs)]
    ppermute x0 -> x35, waiting for transfers between devices: none -> 28.5 us  [swap(): return lax.ppermute(array, axis, pairs)]
    dynamic_slice x32 -> x0, local copies, waits for them, and re-layouts: 16 us -> none  [the longest x24 11.2 us: body(): lax.scan(in_advance, partial_value, (key_rows.reshape(block_count, image_...]
  transfers between devices with their start and end apart: 4 -> 35, of which waited for: 4 -> 11; matrix products, arithmetic and copies ran while one was open for 2% -> 4% of each run, Pallas kernels for 0% -> 6%
where the time goes in v1:
time: 200 us; the launch traced here: 199 us
  Pallas kernels  114 us (57%)
  starting transfers between devices  39.8 us (20%)
  waiting for transfers between devices  28.5 us (14%)
  local copies, waits for them, and re-layouts  10.5 us (5%)
  other arithmetic  5.68 us (3%)
    pallas_call x1, Pallas kernels, attend_call(): pl.pallas_call(functools.partial(attend_kernel, head_dim), grid=(rows //...  55.4 us
    ppermute x35, starting transfers between devices, swap(): return lax.ppermute(array, axis, pairs)  39.8 us
    pallas_call x1, Pallas kernels, render_call(): pl.pallas_call(functools.partial(render_kernel, grid_side, row_span, shar...  31.3 us
    ppermute x35, waiting for transfers between devices, swap(): return lax.ppermute(array, axis, pairs)  28.5 us
    pallas_call x1, Pallas kernels, keys_call(): pl.pallas_call(functools.partial(keys_kernel, len(images)), out_shape=[ja...  8.8 us
    pallas_call x1, Pallas kernels, query_call(): pl.pallas_call(functools.partial(query_kernel, query_scale), grid=(rows /...  7.99 us
    unnamed x65, local copies, waits for them, and re-layouts  7.75 us
    convert_element_type x4, other arithmetic, body(): (kept[j].astype(F32) + swap(passed[j], 'seq', 1).astype(F32)).astype(BF16)  4.72 us
  transfers between devices with their start and end apart: 35, of which 11 were waited for; matrix products, arithmetic and copies ran while one was open for 4% of the time, Pallas kernels for 6%

profile of v1, /device:TPU:1, one launch (start us, length us, event | category | flops | bytes accessed | tf_op | source)
XLA Modules:
  0.0 199.1 jit_solution(8644793722226120919)
XLA Ops:
  0.6 2.1 %collective-permute-start.1 = (bf16[128,768]{1,0:T(8,128)(2,1)}, bf16[128,768]{1,0:T(8,128)(2,1)S(1)}, u32[]{:S(2)}, u32[]{:S(2)}) collective-permute-start(bf16[128,768]{1,0:T(8,128)(2,1)} %bitcast.39), channel_id=1, source_target_pairs={{0,2},{1,3},{2,0},{3,1},{4,6},{5,7},{6,4},{7,5},{8,10},{9,11},{10,... | collective-permute-start | bytes 589832 | tf_op jit(solution)/shard_map/ppermute | solution.py:49
  5.2 2.3 %collective-permute-done.1.refs_2_ = bf16[128,768]{1,0:T(8,128)(2,1)S(1)} collective-permute-done((bf16[128,768]{1,0:T(8,128)(2,1)}, bf16[128,768]{1,0:T(8,128)(2,1)S(1)}, u32[]{:S(2)}, u32[]{:S(2)}) %collective-permute-start.1) | collective-permute-done | bytes 196640 | tf_op jit(solution)/shard_map/ppermute | solution.py:49
  7.6 2.1 %collective-permute-start.2 = (bf16[128,768]{1,0:T(8,128)(2,1)S(1)}, bf16[128,768]{1,0:T(8,128)(2,1)S(1)}, u32[]{:S(2)}, u32[]{:S(2)}) collective-permute-start(bf16[128,768]{1,0:T(8,128)(2,1)S(1)} %collective-permute-done.1.refs_2_), channel_id=1, source_target_pairs={{0,1},{1,0},{2,3},{3,2},{4,5},{5,4},{6,7},{7,6},{8,9},{9,8},{10,11... | collective-permute-start | bytes 589832 | tf_op jit(solution)/shard_map/ppermute | solution.py:49
  9.6 4.8 %collective-permute-start.4 = (bf16[128,768]{1,0:T(8,128)(2,1)S(1)}, bf16[128,768]{1,0:T(8,128)(2,1)S(1)}, u32[]{:S(2)}, u32[]{:S(2)}) collective-permute-start(bf16[128,768]{1,0:T(8,128)(2,1)S(1)} %collective-permute-done.3.refs_4_), channel_id=1, source_target_pairs={{0,1},{1,0},{2,3},{3,2},{4,5},{5,4},{6,7},{7,6},{8,9},{9,8},{10,11... | collective-permute-start | bytes 589832 | tf_op jit(solution)/shard_map/ppermute | solution.py:49
  14.6 8.0 %queries.1.queries_ref = bf16[1536,1024]{1,0:T(8,128)(2,1)} custom-call(bf16[1536,1024]{1,0:T(8,128)(2,1)} %bitcast.33, bf16[1024,1024]{1,0:T(8,128)(2,1)} %w_query_ref.1), custom_call_target="tpu_custom_call" | custom-call | tf_op jit(solution)/shard_map/queries/pallas_call | solution.py:73
  24.1 8.8 %keys_values.1 = (bf16[1024,1024]{1,0:T(8,128)(2,1)}, bf16[8,1024,256]{2,1,0:T(8,128)(2,1)}) custom-call(bf16[128,768]{1,0:T(8,128)(2,1)} %bitcast.43, bf16[128,768]{1,0:T(8,128)(2,1)} %copy-done.13, bf16[128,768]{1,0:T(8,128)(2,1)} %copy-done.10, bf16[128,768]{1,0:T(8,128)(2,1)} %copy-done.14, bf16[128,768]{1,0:T(8,128)(2,1)} %copy-done.11, ...), custom_call_target="tpu_custom_call" | custom-call | tf_op jit(solution)/shard_map/keys_values/pallas_call | solution.py:99
  32.9 55.4 %attention_planes.1 = (bf16[1536,1024]{1,0:T(8,128)(2,1)}, bf16[80,1536]{1,0:T(8,128)(2,1)}) custom-call(bf16[1536,1024]{1,0:T(8,128)(2,1)} %bitcast.34, bf16[1536,1024]{1,0:T(8,128)(2,1)} %queries.1.queries_ref, bf16[1024,1024]{1,0:T(8,128)(2,1)} %get-tuple-element.19.keys_ref, bf16[8,1024,256]{2,1,0:T(8,128)(2,1)} %get-tuple-element.20.values_ref, ...), custom_call_target="tpu_custom_call" | custom-call | tf_op jit(solution)/shard_map/attention_planes/pallas_call | solution.py:159
  92.3 8.7 %collective-permute-done.10.refs_4_ = bf16[80,1536]{1,0:T(8,128)(2,1)S(1)} collective-permute-done((bf16[80,1536]{1,0:T(8,128)(2,1)}, bf16[80,1536]{1,0:T(8,128)(2,1)S(1)}, u32[]{:S(2)}, u32[]{:S(2)}) %collective-permute-start.10) | collective-permute-done | bytes 245792 | tf_op jit(solution)/shard_map/ppermute | solution.py:49
  108.0 31.3 %render.1 = (f32[32,128]{1,0:T(8,128)}, bf16[80,1536]{1,0:T(8,128)(2,1)}, bf16[80,1536]{1,0:T(8,128)(2,1)}, bf16[80,1536]{1,0:T(8,128)(2,1)}, bf16[80,1536]{1,0:...) custom-call(bf16[80,1536]{1,0:T(8,128)(2,1)} %get-tuple-element.21.r, ...), custom_call_target="tpu_custom_call" | custom-call | tf_op jit(solution)/shard_map/render/pallas_call | solution.py:384
  146.9 1.7 add_convert_fusion.refs_3_
  149.5 6.9 %collective-permute-done.17.refs_1_ = bf16[80,1536]{1,0:T(8,128)(2,1)S(1)} collective-permute-done((bf16[80,1536]{1,0:T(8,128)(2,1)S(1)}, bf16[80,1536]{1,0:T(8,128)(2,1)S(1)}, u32[]{:S(2)}, u32[]{:S(2)}) %collective-permute-start.17) | collective-permute-done | bytes 245792 | tf_op jit(solution)/shard_map/ppermute | solution.py:49
  157.2 3.9 %weight_grad.1 = (f32[4,80,128]{2,1,0:T(8,128)}, f32[4,80,128]{2,1,0:T(8,128)}, bf16[80,1536]{1,0:T(8,128)(2,1)}) custom-call(bf16[80,1536]{1,0:T(8,128)(2,1)} %copy-done.2, bf16[80,1536]{1,0:T(8,128)(2,1)} %copy-done.1, bf16[80,1536]{1,0:T(8,128)(2,1)} %copy-done, bf16[80,1536]{1,0:T(8,128)(2,1)} %add_convert_fusion.refs_3_, ...), custom_call_target="tpu_custom_call" | custom-call | tf_op jit(solution)/shard_map/weight_grad/pallas_call | solution.py:441
  161.0 1.3 collective-permute-start.21
  168.3 1.8 collective-permute-done.24
  170.2 1.4 collective-permute-start.25
  171.6 2.3 %collective-permute-start.26 = (f32[80,128]{1,0:T(8,128)S(1)}, f32[80,128]{1,0:T(8,128)S(1)}, u32[]{:S(2)}, u32[]{:S(2)}) collective-permute-start(f32[80,128]{1,0:T(8,128)S(1)} %fusion.2), channel_id=1, source_target_pairs={{0,16},{8,24},{16,0},{24,8},{1,17},{9,25},{17,1},{25,9},{2,18},{10... | collective-permute-start | bytes 122888 | tf_op jit(solution)/shard_map/ppermute | solution.py:49
  173.9 1.9 collective-permute-done.26
  175.7 2.9 %collective-permute-done.27 = f32[80,128]{1,0:T(8,128)S(1)} collective-permute-done((f32[80,128]{1,0:T(8,128)S(1)}, f32[80,128]{1,0:T(8,128)S(1)}, u32[]{:S(2)}, u32[]{:S(2)}) %collective-permute-start.27) | collective-permute-done | bytes 40992 | tf_op jit(solution)/shard_map/ppermute | solution.py:49
  179.8 1.6 collective-permute-start.33
  181.4 4.5 %collective-permute-start.28 = (f32[80,128]{1,0:T(8,128)S(1)}, f32[80,128]{1,0:T(8,128)S(1)}, u32[]{:S(2)}, u32[]{:S(2)}) collective-permute-start(f32[80,128]{1,0:T(8,128)S(1)} %add_add_fusion.refs_0_), channel_id=1, source_target_pairs={{0,1},{1,0},{2,3},{3,2},{4,5},{5,4},{6,7},{7,6},{8,9},{9,8},{10,11... | collective-permute-start | bytes 122888 | tf_op jit(solution)/shard_map/ppermute | solution.py:49
  186.9 2.0 %collective-permute-start.34 = (f32[80,128]{1,0:T(8,128)S(1)}, f32[80,128]{1,0:T(8,128)S(1)}, u32[]{:S(2)}, u32[]{:S(2)}) collective-permute-start(f32[80,128]{1,0:T(8,128)S(1)} %collective-permute-done.33.refs_6_), channel_id=1, source_target_pairs={{0,1},{1,0},{2,3},{3,2},{4,5},{5,4},{6,7},{7,6},{8,9},{9,8},{10,11... | collective-permute-start | bytes 122888 | tf_op jit(solution)/shard_map/ppermute | solution.py:49
  189.6 4.3 %token_grad.1 = bf16[1536,1024]{1,0:T(8,128)(2,1)} custom-call(bf16[80,1536]{1,0:T(8,128)(2,1)} %get-tuple-element.32.grad_ref, bf16[80,1024]{1,0:T(8,128)(2,1)} %bitcast.38), custom_call_target="tpu_custom_call" | custom-call | flops 251658240 | bytes 3145728 | tf_op jit(solution)/shard_map/token_grad/pallas_call | solution.py:462
  195.2 1.9 join_weight_grad.1
  197.1 2.0 copy.26
  (132 shorter events, 34.4 us)
Async XLA Ops:
  0.6 6.9 %collective-permute-start.1 = (bf16[128,768]{1,0:T(8,128)(2,1)}, bf16[128,768]{1,0:T(8,128)(2,1)S(1)}, u32[]{:S(2)}, u32[]{:S(2)}) collective-permute-start(bf16[128,768]{1,0:T(8,128)(2,1)} %bitcast.39), channel_id=1, source_target_pairs={{0,2},{1,3},{2,0},{3,1},{4,6},{5,7},{6,4},{7,5},{8,10},{9,11},{10,... | collective-permute-start | bytes 589832 | tf_op jit(solution)/shard_map/ppermute | solution.py:49
  2.7 6.9 %collective-permute-start.3 = (bf16[128,768]{1,0:T(8,128)(2,1)}, bf16[128,768]{1,0:T(8,128)(2,1)S(1)}, u32[]{:S(2)}, u32[]{:S(2)}) collective-permute-start(bf16[128,768]{1,0:T(8,128)(2,1)} %bitcast.40), channel_id=1, source_target_pairs={{0,4},{1,5},{2,6},{3,7},{4,0},{5,1},{6,2},{7,3},{8,12},{9,13},{10,... | collective-permute-start | bytes 589832 | tf_op jit(solution)/shard_map/ppermute | solution.py:49
  4.0 10.5 %collective-permute-start.5 = (bf16[128,768]{1,0:T(8,128)(2,1)}, bf16[128,768]{1,0:T(8,128)(2,1)S(1)}, u32[]{:S(2)}, u32[]{:S(2)}) collective-permute-start(bf16[128,768]{1,0:T(8,128)(2,1)} %bitcast.41), channel_id=1, source_target_pairs={{0,6},{1,7},{2,4},{3,5},{4,2},{5,3},{6,0},{7,1},{8,14},{9,15},{10,... | collective-permute-start | bytes 589832 | tf_op jit(solution)/shard_map/ppermute | solution.py:49
  4.0 18.6 %collective-permute-start = (bf16[128,768]{1,0:T(8,128)(2,1)}, bf16[128,768]{1,0:T(8,128)(2,1)S(1)}, u32[]{:S(2)}, u32[]{:S(2)}) collective-permute-start(bf16[128,768]{1,0:T(8,128)(2,1)} %bitcast.42), channel_id=1, source_target_pairs={{0,1},{1,0},{2,3},{3,2},{4,5},{5,4},{6,7},{7,6},{8,9},{9,8},{10,11... | collective-permute-start | bytes 589832 | tf_op jit(solution)/shard_map/ppermute | solution.py:49
  7.6 15.0 %collective-permute-start.2 = (bf16[128,768]{1,0:T(8,128)(2,1)S(1)}, bf16[128,768]{1,0:T(8,128)(2,1)S(1)}, u32[]{:S(2)}, u32[]{:S(2)}) collective-permute-start(bf16[128,768]{1,0:T(8,128)(2,1)S(1)} %collective-permute-done.1.refs_2_), channel_id=1, source_target_pairs={{0,1},{1,0},{2,3},{3,2},{4,5},{5,4},{6,7},{7,6},{8,9},{9,8},{10,11... | collective-permute-start | bytes 589832 | tf_op jit(solution)/shard_map/ppermute | solution.py:49
  9.6 13.0 %collective-permute-start.4 = (bf16[128,768]{1,0:T(8,128)(2,1)S(1)}, bf16[128,768]{1,0:T(8,128)(2,1)S(1)}, u32[]{:S(2)}, u32[]{:S(2)}) collective-permute-start(bf16[128,768]{1,0:T(8,128)(2,1)S(1)} %collective-permute-done.3.refs_4_), channel_id=1, source_target_pairs={{0,1},{1,0},{2,3},{3,2},{4,5},{5,4},{6,7},{7,6},{8,9},{9,8},{10,11... | collective-permute-start | bytes 589832 | tf_op jit(solution)/shard_map/ppermute | solution.py:49
  14.5 8.1 %collective-permute-start.6 = (bf16[128,768]{1,0:T(8,128)(2,1)S(1)}, bf16[128,768]{1,0:T(8,128)(2,1)S(1)}, u32[]{:S(2)}, u32[]{:S(2)}) collective-permute-start(bf16[128,768]{1,0:T(8,128)(2,1)S(1)} %collective-permute-done.5.refs_6_), channel_id=1, source_target_pairs={{0,1},{1,0},{2,3},{3,2},{4,5},{5,4},{6,7},{7,6},{8,9},{9,8},{10,11... | collective-permute-start | bytes 589832 | tf_op jit(solution)/shard_map/ppermute | solution.py:49
  88.3 12.6 %collective-permute-start.10 = (bf16[80,1536]{1,0:T(8,128)(2,1)}, bf16[80,1536]{1,0:T(8,128)(2,1)S(1)}, u32[]{:S(2)}, u32[]{:S(2)}) collective-permute-start(bf16[80,1536]{1,0:T(8,128)(2,1)} %get-tuple-element.21.refs_0_), channel_id=1, source_target_pairs={{0,4},{1,5},{2,6},{3,7},{4,0},{5,1},{6,2},{7,3},{8,12},{9,13},{10,... | collective-permute-start | bytes 737288 | tf_op jit(solution)/shard_map/ppermute | solution.py:49
  89.6 12.6 %collective-permute-start.12 = (bf16[80,1536]{1,0:T(8,128)(2,1)}, bf16[80,1536]{1,0:T(8,128)(2,1)S(1)}, u32[]{:S(2)}, u32[]{:S(2)}) collective-permute-start(bf16[80,1536]{1,0:T(8,128)(2,1)} %get-tuple-element.21.refs_0_), channel_id=1, source_target_pairs={{0,6},{1,7},{2,4},{3,5},{4,2},{5,3},{6,0},{7,1},{8,14},{9,15},{10,... | collective-permute-start | bytes 737288 | tf_op jit(solution)/shard_map/ppermute | solution.py:49
  90.4 11.9 %collective-permute-start.8 = (bf16[80,1536]{1,0:T(8,128)(2,1)}, bf16[80,1536]{1,0:T(8,128)(2,1)S(1)}, u32[]{:S(2)}, u32[]{:S(2)}) collective-permute-start(bf16[80,1536]{1,0:T(8,128)(2,1)} %get-tuple-element.21.refs_0_), channel_id=1, source_target_pairs={{0,2},{1,3},{2,0},{3,1},{4,6},{5,7},{6,4},{7,5},{8,10},{9,11},{10,... | collective-permute-start | bytes 737288 | tf_op jit(solution)/shard_map/ppermute | solution.py:49
  91.0 16.0 %collective-permute-start.7 = (bf16[80,1536]{1,0:T(8,128)(2,1)}, bf16[80,1536]{1,0:T(8,128)(2,1)S(1)}, u32[]{:S(2)}, u32[]{:S(2)}) collective-permute-start(bf16[80,1536]{1,0:T(8,128)(2,1)} %get-tuple-element.21.refs_0_), channel_id=1, source_target_pairs={{0,1},{1,0},{2,3},{3,2},{4,5},{5,4},{6,7},{7,6},{8,9},{9,8},{10,11... | collective-permute-start | bytes 737288 | tf_op jit(solution)/shard_map/ppermute | solution.py:49
  100.9 6.1 %collective-permute-start.11 = (bf16[80,1536]{1,0:T(8,128)(2,1)S(1)}, bf16[80,1536]{1,0:T(8,128)(2,1)S(1)}, u32[]{:S(2)}, u32[]{:S(2)}) collective-permute-start(bf16[80,1536]{1,0:T(8,128)(2,1)S(1)} %collective-permute-done.10.refs_4_), channel_id=1, source_target_pairs={{0,1},{1,0},{2,3},{3,2},{4,5},{5,4},{6,7},{7,6},{8,9},{9,8},{10,11... | collective-permute-start | bytes 737288 | tf_op jit(solution)/shard_map/ppermute | solution.py:49
  102.2 4.9 %collective-permute-start.13 = (bf16[80,1536]{1,0:T(8,128)(2,1)S(1)}, bf16[80,1536]{1,0:T(8,128)(2,1)S(1)}, u32[]{:S(2)}, u32[]{:S(2)}) collective-permute-start(bf16[80,1536]{1,0:T(8,128)(2,1)S(1)} %collective-permute-done.12.refs_6_), channel_id=1, source_target_pairs={{0,1},{1,0},{2,3},{3,2},{4,5},{5,4},{6,7},{7,6},{8,9},{9,8},{10,11... | collective-permute-start | bytes 737288 | tf_op jit(solution)/shard_map/ppermute | solution.py:49
  139.3 7.6 %collective-permute-start.20 = (bf16[80,1536]{1,0:T(8,128)(2,1)}, bf16[80,1536]{1,0:T(8,128)(2,1)S(1)}, u32[]{:S(2)}, u32[]{:S(2)}) collective-permute-start(bf16[80,1536]{1,0:T(8,128)(2,1)} %get-tuple-element.30), channel_id=1, source_target_pairs={{0,1},{1,0},{2,3},{3,2},{4,5},{5,4},{6,7},{7,6},{8,9},{9,8},{10,11... | collective-permute-start | bytes 737288 | tf_op jit(solution)/shard_map/ppermute | solution.py:49
  142.0 7.5 %collective-permute-start.19 = (bf16[80,1536]{1,0:T(8,128)(2,1)S(1)}, bf16[80,1536]{1,0:T(8,128)(2,1)S(1)}, u32[]{:S(2)}, u32[]{:S(2)}) collective-permute-start(bf16[80,1536]{1,0:T(8,128)(2,1)S(1)} %add_convert_fusion.1), channel_id=1, source_target_pairs={{0,2},{1,3},{2,0},{3,1},{4,6},{5,7},{6,4},{7,5},{8,10},{9,11},{10,... | collective-permute-start | bytes 737288 | tf_op jit(solution)/shard_map/ppermute | solution.py:49
  144.0 12.4 %collective-permute-start.17 = (bf16[80,1536]{1,0:T(8,128)(2,1)S(1)}, bf16[80,1536]{1,0:T(8,128)(2,1)S(1)}, u32[]{:S(2)}, u32[]{:S(2)}) collective-permute-start(bf16[80,1536]{1,0:T(8,128)(2,1)S(1)} %add_convert_fusion.2), channel_id=1, source_target_pairs={{0,4},{1,5},{2,6},{3,7},{4,0},{5,1},{6,2},{7,3},{8,12},{9,13},{10,... | collective-permute-start | bytes 737288 | tf_op jit(solution)/shard_map/ppermute | solution.py:49
  145.7 10.7 %collective-permute-start.15 = (bf16[80,1536]{1,0:T(8,128)(2,1)S(1)}, bf16[80,1536]{1,0:T(8,128)(2,1)S(1)}, u32[]{:S(2)}, u32[]{:S(2)}) collective-permute-start(bf16[80,1536]{1,0:T(8,128)(2,1)S(1)} %add_convert_fusion.3), channel_id=1, source_target_pairs={{0,6},{1,7},{2,4},{3,5},{4,2},{5,3},{6,0},{7,1},{8,14},{9,15},{10,... | collective-permute-start | bytes 737288 | tf_op jit(solution)/shard_map/ppermute | solution.py:49
  178.7 7.2 %collective-permute-start.29 = (f32[80,128]{1,0:T(8,128)S(1)}, f32[80,128]{1,0:T(8,128)S(1)}, u32[]{:S(2)}, u32[]{:S(2)}) collective-permute-start(f32[80,128]{1,0:T(8,128)S(1)} %add_add_fusion.refs_0_), channel_id=1, source_target_pairs={{0,2},{1,3},{2,0},{3,1},{4,6},{5,7},{6,4},{7,5},{8,10},{9,11},{10,... | collective-permute-start | bytes 122888 | tf_op jit(solution)/shard_map/ppermute | solution.py:49
  179.0 7.4 %collective-permute-start.31 = (f32[80,128]{1,0:T(8,128)S(1)}, f32[80,128]{1,0:T(8,128)S(1)}, u32[]{:S(2)}, u32[]{:S(2)}) collective-permute-start(f32[80,128]{1,0:T(8,128)S(1)} %add_add_fusion.refs_0_), channel_id=1, source_target_pairs={{0,4},{1,5},{2,6},{3,7},{4,0},{5,1},{6,2},{7,3},{8,12},{9,13},{10,... | collective-permute-start | bytes 122888 | tf_op jit(solution)/shard_map/ppermute | solution.py:49
  179.8 7.1 %collective-permute-start.33 = (f32[80,128]{1,0:T(8,128)S(1)}, f32[80,128]{1,0:T(8,128)S(1)}, u32[]{:S(2)}, u32[]{:S(2)}) collective-permute-start(f32[80,128]{1,0:T(8,128)S(1)} %add_add_fusion.refs_0_), channel_id=1, source_target_pairs={{0,6},{1,7},{2,4},{3,5},{4,2},{5,3},{6,0},{7,1},{8,14},{9,15},{10,... | collective-permute-start | bytes 122888 | tf_op jit(solution)/shard_map/ppermute | solution.py:49
  181.4 12.5 %collective-permute-start.28 = (f32[80,128]{1,0:T(8,128)S(1)}, f32[80,128]{1,0:T(8,128)S(1)}, u32[]{:S(2)}, u32[]{:S(2)}) collective-permute-start(f32[80,128]{1,0:T(8,128)S(1)} %add_add_fusion.refs_0_), channel_id=1, source_target_pairs={{0,1},{1,0},{2,3},{3,2},{4,5},{5,4},{6,7},{7,6},{8,9},{9,8},{10,11... | collective-permute-start | bytes 122888 | tf_op jit(solution)/shard_map/ppermute | solution.py:49
  185.9 8.0 %collective-permute-start.30 = (f32[80,128]{1,0:T(8,128)S(1)}, f32[80,128]{1,0:T(8,128)S(1)}, u32[]{:S(2)}, u32[]{:S(2)}) collective-permute-start(f32[80,128]{1,0:T(8,128)S(1)} %collective-permute-done.29.refs_2_), channel_id=1, source_target_pairs={{0,1},{1,0},{2,3},{3,2},{4,5},{5,4},{6,7},{7,6},{8,9},{9,8},{10,11... | collective-permute-start | bytes 122888 | tf_op jit(solution)/shard_map/ppermute | solution.py:49
  186.4 7.5 %collective-permute-start.32 = (f32[80,128]{1,0:T(8,128)S(1)}, f32[80,128]{1,0:T(8,128)S(1)}, u32[]{:S(2)}, u32[]{:S(2)}) collective-permute-start(f32[80,128]{1,0:T(8,128)S(1)} %collective-permute-done.31.refs_4_), channel_id=1, source_target_pairs={{0,1},{1,0},{2,3},{3,2},{4,5},{5,4},{6,7},{7,6},{8,9},{9,8},{10,11... | collective-permute-start | bytes 122888 | tf_op jit(solution)/shard_map/ppermute | solution.py:49
  186.9 7.0 %collective-permute-start.34 = (f32[80,128]{1,0:T(8,128)S(1)}, f32[80,128]{1,0:T(8,128)S(1)}, u32[]{:S(2)}, u32[]{:S(2)}) collective-permute-start(f32[80,128]{1,0:T(8,128)S(1)} %collective-permute-done.33.refs_6_), channel_id=1, source_target_pairs={{0,1},{1,0},{2,3},{3,2},{4,5},{5,4},{6,7},{7,6},{8,9},{9,8},{10,11... | collective-permute-start | bytes 122888 | tf_op jit(solution)/shard_map/ppermute | solution.py:49
  (42 other events, 549.2 us)
